TPU v7x, 32 devices: a whole 2x2x4 slice. The times are simulated.
32 devices in a mesh: dp: 16 (over z, y, core), seq: 2 (over x).
Axes of the slice: x: 2, y: 2, z: 4, core: 2. Of those that a mesh axis runs over, the one named last changes fastest.
Arguments:
- checkpoint: bfloat16 [16384, 8192], P(('dp', 'seq')), may hold values from -6 to 6
- norm_gain: float32 [8192], replicated, may hold values from 0.1 to 1.9
- key_cotangent: bfloat16 [16384, 1024], P(('dp', 'seq')), may hold values from -6 to 6
- positions: int32 [16384], P(('dp', 'seq')), may hold values from 0 to 4095, as said below
- kept_cols: int32 [128, 6], replicated, may hold values from 0 to 15, as said below
- kept_count: int32 [128], replicated, may hold values from 2 to 6
- key_blocks: bfloat16 [128, 6, 4096], P('dp'), may hold values from -0.375 to 0.375
Outputs:
- input_grad: bfloat16 [16384, 8192], P(('dp', 'seq'))
- block_grad: float32 [128, 6, 4096], P('dp', None, 'seq')
Inputs may be any that keep to these rules, and one draw needn't show every extreme that they name: `kept_cols`: the 6 entries of a row are different block columns; only the first kept_count entries of a row name kept blocks, the others are unused slots. Inside a document the positions rise by one from token to token.
All inputs are finite; a program needn't handle non-finite values.
Results may differ from a plain program's by a relative error of at most 0.0049.
Values may be sent and summed in bfloat16 or wider, within the bound.
A program may use at most 128 MiB of HBM per device.

v0:
```python
import math

import jax
import jax.numpy as jnp
from jax import lax
from jax.sharding import PartitionSpec as P

D = 8192
KVW = 1024
HEAD_DIM = 128
BLK = 64
MOSTR = 6
SEQ_LEN = 1024


def rope_back(grad, positions):
    heads = KVW // HEAD_DIM
    half = HEAD_DIM // 2
    values = grad.astype(jnp.float32).reshape(-1, heads, 2, half)
    freqs = 10000.0 ** (-2.0 * jnp.arange(half).astype(jnp.float32) / HEAD_DIM)
    angle = positions.astype(jnp.float32)[:, None] * freqs[None, :]
    cosine = jnp.cos(angle)[:, None, :]
    sine = jnp.sin(angle)[:, None, :]
    first = values[:, :, 0] * cosine + values[:, :, 1] * sine
    second = values[:, :, 1] * cosine - values[:, :, 0] * sine
    return jnp.stack([first, second], axis=2).reshape(-1, KVW).astype(jnp.bfloat16)


def densify(blocks, cols, count, rows):
    count_rows = blocks.shape[0]
    col_blocks = KVW // BLK
    slot_ids = lax.broadcasted_iota(jnp.int32, (count_rows, MOSTR), 1)
    live = slot_ids < count[:, None]
    col_ids = lax.broadcasted_iota(jnp.int32, (count_rows, MOSTR, col_blocks), 2)
    onehot = ((cols[:, :, None] == col_ids) & live[:, :, None]).astype(jnp.bfloat16)
    placed = lax.dot_general(
        onehot, blocks, (((1,), (1,)), ((0,), (0,))), preferred_element_type=jnp.bfloat16
    )
    dense = placed.reshape(count_rows, col_blocks, rows, BLK).transpose(0, 2, 1, 3)
    return dense.reshape(count_rows * rows, KVW)


def shards(checkpoint, norm_gain, key_cotangent, positions, kept_cols, kept_count, key_blocks):
    tok_rows = checkpoint.shape[0]
    groups = lax.axis_size("seq")
    part_rows = BLK // groups
    row_blocks = D // BLK
    col_blocks = KVW // BLK
    xf = checkpoint.astype(jnp.float32)
    inv_rms = lax.rsqrt(jnp.mean(xf * xf, axis=1, keepdims=True) + 1e-05)
    normed = (xf * inv_rms * norm_gain).astype(jnp.bfloat16)
    grad_pre = rope_back(key_cotangent, positions)
    grad_all = lax.all_gather(grad_pre, "seq", axis=0, tiled=True)
    split_normed = (
        normed.reshape(tok_rows, row_blocks, groups, part_rows)
        .transpose(0, 2, 1, 3)
        .reshape(tok_rows, groups, row_blocks * part_rows)
    )
    received = lax.all_to_all(split_normed, "seq", split_axis=1, concat_axis=0, tiled=True)
    normed_rows = received.reshape(groups * tok_rows, row_blocks, part_rows)
    divisor = math.sqrt(SEQ_LEN * lax.axis_size("dp"))
    count = row_blocks // lax.axis_size("dp") * lax.axis_size("dp")
    slab = normed_rows.reshape(groups * tok_rows, count * part_rows)
    product = lax.dot_general(
        slab, grad_all, (((0,), (0,)), ((), ())), preferred_element_type=jnp.float32
    )
    shaped = (
        product.reshape(count, part_rows, col_blocks, BLK)
        .transpose(0, 2, 1, 3)
        .reshape(count, col_blocks, part_rows * BLK)
    )
    cols = kept_cols
    counts = kept_count
    picked = jnp.take_along_axis(shaped, cols[:, :, None], axis=1)
    live = lax.broadcasted_iota(jnp.int32, (count, MOSTR), 1) < counts[:, None]
    block_grad = lax.psum_scatter(
        jnp.where(live[:, :, None], picked / divisor, jnp.float32(0.0)),
        "dp",
        scatter_dimension=0,
        tiled=True,
    )
    piece = lax.all_gather(key_blocks, "dp", axis=0, tiled=True)
    cols = kept_cols
    counts = kept_count
    dense = densify(piece, cols, counts, BLK)
    normed_grad = lax.dot_general(
        grad_pre, dense, (((1,), (1,)), ((), ())), preferred_element_type=jnp.float32
    )
    scaled = norm_gain * normed_grad
    grads = inv_rms * scaled - inv_rms**3 * xf * jnp.mean(scaled * xf, axis=1, keepdims=True)
    return (grads.astype(jnp.bfloat16), block_grad)


def solution(mesh):
    placed = (
        P(("dp", "seq"), None),
        P(),
        P(("dp", "seq"), None),
        P(("dp", "seq")),
        P(),
        P(),
        P("dp", None, None),
    )
    return jax.shard_map(
        shards,
        mesh=mesh,
        in_specs=placed,
        out_specs=(P(("dp", "seq"), None), P("dp", None, "seq")),
        check_vma=False,
    )
```

profile of v0, /device:TPU:0, one launch (start us, length us, event | category | flops | bytes accessed | tf_op | source)
XLA Modules:
  0.0 589.4 jit_solution(2755816702823325204)
XLA Ops:
  8.1 0.7 all-gather.3.cloned.1.call-update
  8.7 0.7 convert_element_type.35
  9.4 1.5 copy.29
  10.9 0.3 convert.1
  11.2 0.8 copy.30
  12.0 0.5 multiply_cosine_fusion
  12.6 0.3 multiply_add_fusion
  13.1 62.6 %all-gather.3.cloned.1.call-done = bf16[128,6,4096]{2,0,1:T(8,128)(2,1)} async-done(((bf16[8,6,4096]{2,0,1:T(8,128)(2,1)}), bf16[128,6,4096]{2,0,1:T(8,128)(2,1)}) %all-gather.3.cloned.1.call-update) | async-done | bytes 6291472 | tf_op jit(solution)/shard_map/all_gather | solution.py:82
  75.7 16.3 %fusion.8 = bf16[128,16,4096]{2,1,0:T(8,128)(2,1)} fusion(bf16[128,6,4096]{2,0,1:T(8,128)(2,1)} %all-gather.3.cloned.1.call-done, s32[128,6]{1,0:T(8,128)S(1)} %copy.30, pred[128,6]{1,0:T(8,128)(4,1)S(1)} %iota_compare_fusion.1), kind=kOutput, calls=%fused_computation.14 | convolution fusion | flops 100687872 | bytes 23072512 | tf_op jit(solution)/shard_map/dot_general | solution.py:36
  92.0 22.5 %copy.32 = bf16[128,16,4096]{0,2,1:T(8,128)(2,1)} copy(bf16[128,16,4096]{2,1,0:T(8,128)(2,1)} %fusion.8) | data formatting | bytes 33554432 | tf_op jit(solution)/shard_map/dot_general | solution.py:36
  114.5 46.0 %copy.33 = bf16[128,64,16,64]{3,2,1,0:T(8,128)(2,1)} copy(bf16[128,64,16,64]{0,3,1,2:T(8,128)(2,1)} %bitcast.36) | data formatting | bytes 33554432 | tf_op jit(solution)/shard_map/transpose | solution.py:39
  160.5 44.1 %reshape.139 = bf16[8192,1024]{1,0:T(8,128)(2,1)} reshape(bf16[128,64,16,64]{3,2,1,0:T(8,128)(2,1)} %copy.33) | data formatting | bytes 33554432 | tf_op jit(solution)/shard_map/reshape | solution.py:40
  204.6 18.8 %fusion = (f32[512]{0:T(512)S(1)}, f32[512]{0:T(512)S(1)}, f32[512,8192]{1,0:T(8,128)}) fusion(bf16[512,8192]{1,0:T(8,128)(2,1)} %param.7, f32[8192]{0:T(1024)S(1)} %copy-done.4, bf16[512,1024]{0,1:T(8,128)(2,1)S(1)} %bitcast.43, bf16[8192,1024]{1,0:T(8,128)(2,1)} %reshape.139), kind=kOutput, calls=%fused_computation.5 | convolution fusion | flops 8615100416 | bytes 43028480 | tf_op jit(solution)/shard_map/dot_general | solution.py:86
  223.5 16.2 %fusion.6 = (bf16[512,8192]{1,0:T(8,128)(2,1)}, bf16[512,8192]{1,0:T(8,128)(2,1)}) fusion(bf16[512,8192]{1,0:T(8,128)(2,1)} %param.7, f32[8192]{0:T(1024)S(1)} %copy-done.4, f32[512]{0:T(512)S(1)} %get-tuple-element.14, f32[512]{0:T(512)S(1)} %get-tuple-element.17, f32[512]{0:T(512)S(1)} %get-tuple-element.15, f32[512,8192]{1,0:T(8,128)} %get-tuple-element.16), kind=kLoop, calls=%fused_computation.11 | loop fusion | flops 41943040 | bytes 41981952 | tf_op jit(solution)/shard_map/convert_element_type | solution.py:51
  239.7 12.0 %copy.35 = bf16[512,8192]{0,1:T(8,128)(2,1)} copy(bf16[512,8192]{1,0:T(8,128)(2,1)} %get-tuple-element.8) | data formatting | bytes 16777216 | tf_op jit(solution)/shard_map/convert_element_type | solution.py:51
  251.7 8.3 %copy.36 = bf16[512,2,128,32]{0,3,2,1:T(8,128)(2,1)} copy(bf16[512,2,128,32]{0,3,1,2:T(8,128)(2,1)} %bitcast.39) | data formatting | bytes 16777216 | tf_op jit(solution)/shard_map/transpose | solution.py:56
  259.9 7.1 %all-to-all-start = ((bf16[512,2,4096]{0,2,1:T(8,128)(2,1)}), bf16[512,2,4096]{0,2,1:T(8,128)(2,1)}, u32[]{:S(2)}, u32[]{:S(2)}) async-start(bf16[512,2,4096]{0,2,1:T(8,128)(2,1)} %bitcast.38), calls=%async_computation | async-start | bytes 16777216 | tf_op jit(solution)/shard_map/all_to_all | solution.py:59
  267.1 0.5 all-gather.5.cloned.1.call-update
  267.7 0.1 copy.41
  267.8 0.1 reshape.145
  267.9 0.1 copy.34
  268.1 114.4 %all-to-all-done = bf16[512,2,4096]{0,2,1:T(8,128)(2,1)} async-done(((bf16[512,2,4096]{0,2,1:T(8,128)(2,1)}), bf16[512,2,4096]{0,2,1:T(8,128)(2,1)}, u32[]{:S(2)}, u32[]{:S(2)}) %all-to-all-start) | async-done | bytes 8388640 | tf_op jit(solution)/shard_map/all_to_all | solution.py:59
  382.5 12.0 %copy.37 = bf16[2,512,1,4096]{3,1,0,2:T(8,128)(2,1)} copy(bf16[2,512,1,4096]{1,3,0,2:T(8,128)(2,1)} %bitcast.9) | data formatting | bytes 16777216 | tf_op jit(solution)/shard_map/all_to_all | solution.py:59
  394.5 12.0 %copy.38 = bf16[4096,1024]{1,0:T(8,128)(2,1)} copy(bf16[4096,1024]{0,1:T(8,128)(2,1)} %bitcast.40) | data formatting | bytes 16777216 | tf_op jit(solution)/shard_map/dot_general | solution.py:64
  406.5 17.1 %convolution_bitcast_fusion = f32[128,16,32,64]{0,3,1,2:T(8,128)S(1)} fusion(bf16[16,64,1024,1]{2,1,0,3:T(8,128)(2,1)} %bitcast.45, bf16[128,32,1024,1]{2,1,0,3:T(8,128)(2,1)} %bitcast.41), kind=kOutput, calls=%fused_computation.12 | convolution fusion | flops 8589934592 | bytes 27262976 | tf_op jit(solution)/shard_map/dot_general | solution.py:64
  423.6 6.5 %copy.40 = f32[128,16,32,64]{0,3,2,1:T(8,128)} copy(f32[128,16,32,64]{0,3,1,2:T(8,128)S(1)} %convolution_bitcast_fusion) | data formatting | bytes 33554432 | tf_op jit(solution)/shard_map/transpose | solution.py:69
  430.1 18.2 %copy.42 = f32[128,16,2048]{2,1,0:T(8,128)} copy(f32[128,16,2048]{0,2,1:T(8,128)} %bitcast.37) | data formatting | bytes 33554432 | tf_op jit(solution)/shard_map/reshape | solution.py:70
  448.4 15.1 %gather_fusion = f32[768,2048]{1,0:T(8,128)} fusion(f32[128,16,2048]{2,1,0:T(8,128)} %copy.42, s32[768]{0:T(1024)S(1)} %reshape.145), kind=kCustom, calls=%fused_computation | custom fusion | bytes 12589056 | tf_op jit(solution)/shard_map/jit(take_along_axis)/gather | solution.py:74
  463.4 7.9 %reshape.148 = f32[128,6,2048]{2,1,0:T(8,128)} reshape(f32[768,2048]{1,0:T(8,128)} %gather_fusion) | data formatting | bytes 12582912 | tf_op jit(solution)/shard_map/jit(take_along_axis)/gather | solution.py:74
  471.3 6.1 %multiply_select_fusion = f32[128,6,2048]{2,1,0:T(8,128)} fusion(f32[128,6,2048]{2,1,0:T(8,128)} %reshape.148, pred[128,6]{1,0:T(8,128)(4,1)S(1)} %copy.34, pred[128,6]{1,0:T(8,128)(4,1)S(1)} %copy-done.2), kind=kLoop, calls=%fused_computation.16 | loop fusion | flops 4718592 | bytes 12584448 | tf_op jit(solution)/shard_map/jit(_where)/select_n | solution.py:77
  477.4 102.5 %reduce-scatter.2.cloned.1.call-done = f32[8,6,2048]{2,1,0:T(8,128)} async-done(((f32[128,6,2048]{2,1,0:T(8,128)}), f32[8,6,2048]{2,1,0:T(8,128)}) %reduce-scatter.2.cloned.1.call-update) | async-done | bytes 393232 | tf_op jit(solution)/shard_map/reduce_scatter | solution.py:76
  579.9 2.0 copy.43
  (23 shorter events, 0.4 us)
Async XLA Ops:
  8.0 5.0 copy-start.5
  8.0 67.7 %all-gather.3.cloned.1.call-start = ((), (), s32[]{:S(2)}) async-start(), calls=%async_computation.2 | async-start | bytes 6684672 | tf_op jit(solution)/shard_map/all_gather | solution.py:82
  13.0 191.6 %copy-start = (bf16[512,8,2,64]{0,3,2,1:T(8,128)(2,1)}, bf16[512,8,2,64]{0,3,2,1:T(8,128)(2,1)S(1)}, u32[]{:S(2)}) copy-start(bf16[512,8,2,64]{0,3,2,1:T(8,128)(2,1)S(1)} %maximum_convert_fusion) | copy-start | bytes 3145732
  13.1 78.9 %copy-start.1 = (pred[128,6]{1,0:T(8,128)(4,1)}, pred[128,6]{1,0:T(8,128)(4,1)S(1)}, u32[]{:S(2)}) copy-start(pred[128,6]{1,0:T(8,128)(4,1)S(1)} %iota_compare_fusion.1) | copy-start | bytes 2308
  160.5 44.1 %copy-start.4 = (f32[8192]{0:T(1024)S(1)}, f32[8192]{0:T(1024)}, u32[]{:S(2)}) copy-start(f32[8192]{0:T(1024)} %param.8) | copy-start | bytes 98308
  259.9 7.7 %copy-start.3 = (s32[128,6]{0,1:T(8,128)S(1)}, s32[128,6]{0,1:T(8,128)}, u32[]{:S(2)}) copy-start(s32[128,6]{0,1:T(8,128)} %param.11) | copy-start | bytes 9220
  259.9 122.6 %all-to-all-start = ((bf16[512,2,4096]{0,2,1:T(8,128)(2,1)}), bf16[512,2,4096]{0,2,1:T(8,128)(2,1)}, u32[]{:S(2)}, u32[]{:S(2)}) async-start(bf16[512,2,4096]{0,2,1:T(8,128)(2,1)} %bitcast.38), calls=%async_computation | async-start | bytes 16777216 | tf_op jit(solution)/shard_map/all_to_all | solution.py:59
  267.0 139.5 %all-gather.5.cloned.1.call-start = ((), (), s32[]{:S(2)}) async-start(), calls=%async_computation.3 | async-start | bytes 3145728 | tf_op jit(solution)/shard_map/all_gather | solution.py:53
  267.6 312.3 %reduce-scatter.2.cloned.1.call-start = ((), (), s32[]{:S(2)}) async-start(), calls=%async_computation.4 | async-start | bytes 8912896 | tf_op jit(solution)/shard_map/reduce_scatter | solution.py:76
  463.4 7.9 %copy-start.2 = (pred[128,6]{1,0:T(8,128)(4,1)S(1)}, pred[128,6]{1,0:T(8,128)(4,1)}, u32[]{:S(2)}) copy-start(pred[128,6]{1,0:T(8,128)(4,1)} %copy-done.1) | copy-start | bytes 2308
Sparse Core Ops, SparseCore 0:
  11.0 64.6 all-gather.2
  477.6 102.3 reduce-scatter.1
Sparse Core Ops, SparseCore 1:
  269.0 54.7 all-gather.4
where the time goes:
time: 594 us; the launch traced here: 589 us
  waiting for transfers between devices  281 us (47%)
  local copies, waits for them, and re-layouts  209 us (35%)
  matrix products  52.3 us (9%)
  other arithmetic  24.4 us (4%)
  between operations  15.6 us (3%)
  starting transfers between devices  7.2 us (1%)
    all_to_all x1, waiting for transfers between devices, shards(): lax.all_to_all(split_normed, 'seq', split_axis=1, concat_axis=0, tiled=True)  114 us
    reduce_scatter x1, waiting for transfers between devices, shards(): lax.psum_scatter(jnp.where(live[:, :, None], picked / divisor, jnp.float3...  102 us
    all_gather x1, waiting for transfers between devices, shards(): piece = lax.all_gather(key_blocks, 'dp', axis=0, tiled=True)  62.6 us
    transpose x1, local copies, waits for them, and re-layouts, densify(): placed.reshape(count_rows, col_blocks, rows, BLK).transpose(0, 2, 1, 3)  46 us
    reshape x1, local copies, waits for them, and re-layouts, densify(): return dense.reshape(count_rows * rows, KVW)  44.1 us
    gather x4, local copies, waits for them, and re-layouts, shards(): picked = jnp.take_along_axis(shaped, cols[:, :, None], axis=1)  23.2 us
    dot_general x1, local copies, waits for them, and re-layouts, densify(): lax.dot_general(onehot, blocks, (((1,), (1,)), ((0,), (0,))), preferred_e...  22.5 us
    dot_general x1, matrix products, shards(): lax.dot_general(grad_pre, dense, (((1,), (1,)), ((), ())), preferred_elem...  18.8 us
  transfers between devices with their start and end apart: 4, of which 3 were waited for; matrix products, arithmetic and copies ran while one was open for 5% of the time, Pallas kernels for 0%

commit v1 on v0

v1 whole, which is shorter than its diff:
```python
import functools
import math

import jax
import jax.numpy as jnp
from jax import lax
from jax.experimental import pallas as pl
from jax.experimental.pallas import tpu as pltpu
from jax.sharding import PartitionSpec as P

D = 8192
KVW = 1024
HEAD_DIM = 128
BLK = 64
MOSTR = 6
SEQ_LEN = 1024
STREAMS = MOSTR // 2
LANES = 128
VMEM = 58 * 1024 * 1024


def bits_of(n):
    return int(math.log2(n))


def stage_plan(dp, seq):
    low = ("dp", 0)
    high = [("dp", b) for b in range(1, bits_of(dp))]
    seqs = [("seq", b) for b in range(bits_of(seq))]
    if dp == 16 and seq == 2:
        y, z1, z2 = high
        (x,) = seqs
        return [[low, x, y, z1, z2], [low, y, x, z1, z2], [low, z1, z2, x, y]]
    return [[low] + seqs + high, [low] + high + seqs, [low] + high[::-1] + seqs]


def bit(value, b):
    return (value // (1 << b)) % 2


def slot_of(order, dp_index, seq_index):
    place = 0
    for axis, b in order[1:]:
        place = place * 2 + bit(dp_index if axis == "dp" else seq_index, b)
    return place


def sums_kernel(dp, seq, x_ref, gain_ref, cot_ref, cos_ref, sin_ref, cols_ref,
                pre_ref, inv_ref, fin_ref,
                sums, first, acc, later, recv_first, recv_later, send_sem, recv_sem):
    tokens = x_ref.shape[0]
    rows_dp = (D // BLK) // dp
    part = BLK // seq
    tile = rows_dp * BLK
    plan = stage_plan(dp, seq)
    stages = len(plan[0])
    me_dp = lax.axis_index("dp")
    me_seq = lax.axis_index("seq")

    def partner(axis, b):
        mine = me_dp if axis == "dp" else me_seq
        other = mine + (1 << b) - 2 * (1 << b) * bit(mine, b)
        return (other, me_seq) if axis == "dp" else (me_dp, other)

    def mybit(axis, b):
        return bit(me_dp if axis == "dp" else me_seq, b)

    barrier = pltpu.get_barrier_semaphore()
    for axis, b in plan[0]:
        pl.semaphore_signal(barrier, inc=1, device_id=partner(axis, b),
                            device_id_type=pl.DeviceIdType.MESH)
    pl.semaphore_wait(barrier, stages)

    tt = 64

    @pl.loop(0, tokens // tt)
    def _(t):
        rows = pl.ds(pl.multiple_of(t * tt, tt), tt)
        total = jnp.zeros((tt, LANES), jnp.float32)
        for j in range(D // LANES):
            v = x_ref[rows, j * LANES:(j + 1) * LANES].astype(jnp.float32)
            total = total + v * v
        mean = jnp.sum(total, axis=1, keepdims=True) / D
        inv_ref[rows, :] = jnp.broadcast_to(lax.rsqrt(mean + 1e-05), (tt, LANES))
        cosine = cos_ref[rows, :]
        sine = sin_ref[rows, :]
        for h in range(KVW // HEAD_DIM):
            v = cot_ref[rows, h * HEAD_DIM:(h + 1) * HEAD_DIM].astype(jnp.float32)
            pre_ref[rows, h * HEAD_DIM:(h + 1) * HEAD_DIM] = (
                v * cosine + pltpu.roll(v, HEAD_DIM // 2, 1) * sine
            ).astype(jnp.bfloat16)

    lane = lax.broadcasted_iota(jnp.int32, (BLK, LANES), 1)

    def one_owner(owner, store):
        start = pl.multiple_of(owner * tile, tile)
        inv = inv_ref[:, :1]
        normed = (
            x_ref[:, pl.ds(start, tile)].astype(jnp.float32) * inv
            * gain_ref[:, pl.ds(start, tile)]
        ).astype(jnp.bfloat16)
        for n in range(KVW // 256):
            product = lax.dot_general(
                normed, pre_ref[:, n * 256:(n + 1) * 256], (((0,), (0,)), ((), ())),
                preferred_element_type=jnp.float32,
            )
            sums[2 * n] = product[:, :LANES]
            sums[2 * n + 1] = product[:, LANES:]
        for s in range(STREAMS):
            for pair in range(rows_dp // 2):
                both = []
                for j in (2 * pair, 2 * pair + 1):
                    halves = []
                    for k in (2 * s, 2 * s + 1):
                        col = cols_ref[owner * rows_dp + j, k]
                        v = sums[col // 2, j * BLK:(j + 1) * BLK, :]
                        halves.append(pltpu.roll(v, ((col + k) % 2) * BLK, 1))
                    both.append(jnp.where(lane < BLK, halves[0], halves[1]))
                for q in range(seq):
                    v = jnp.concatenate([w[q * part:(q + 1) * part] for w in both], axis=0)
                    store(s, slot_of(plan[s], owner, q), 2 * part * pair, v)

    def exchange(s, i, size):
        axis, b = plan[s][i]
        if i == 0:
            src, dst = first.at[s], recv_first.at[s]
        else:
            begin = recv_later.shape[1] - 2 * size + 0
            src = later.at[s, pl.ds(begin, size)]
            dst = recv_later.at[s, pl.ds(begin, size)]
        return pltpu.make_async_remote_copy(
            src_ref=src, dst_ref=dst, send_sem=send_sem.at[s, i], recv_sem=recv_sem.at[s, i],
            device_id=partner(axis, b), device_id_type=pl.DeviceIdType.MESH,
        )

    mine = me_dp % 2
    half = dp * seq // 2

    @pl.loop(0, dp // 2)
    def _(o):
        def store(s, slot, row, v):
            first[s, slot, row:row + 2 * part, :] = v.astype(jnp.bfloat16)

        one_owner(2 * o + 1 - mine, store)

    copies = {}
    for s in range(STREAMS):
        copies[s, 0] = exchange(s, 0, half)
        copies[s, 0].start()

    @pl.loop(0, dp // 2)
    def _(o):
        def store(s, slot, row, v):
            acc[s, slot, row:row + 2 * part, :] = v

        one_owner(2 * o + mine, store)

    base = [0] * STREAMS
    for i in range(stages):
        size = half >> i
        for s in range(STREAMS):
            copies[s, i].wait()
            got = recv_first.at[s] if i == 0 else recv_later.at[
                s, pl.ds(recv_later.shape[1] - 2 * size, size)]
            if i == stages - 1:
                fin_ref[s] = acc[s, base[s]] + got[0].astype(jnp.float32)
                continue
            axis, b = plan[s][i + 1]
            keep = mybit(axis, b)
            h = size // 2
            give = (1 - keep) * h
            where = recv_later.shape[1] - 2 * h

            @pl.loop(0, h)
            def _(t):
                v = acc[s, base[s] + give + t] + got[give + t].astype(jnp.float32)
                later[s, where + t] = v.astype(jnp.bfloat16)

            copies[s, i + 1] = exchange(s, i + 1, h)
            copies[s, i + 1].start()

            @pl.loop(0, h)
            def _(t):
                at = base[s] + keep * h + t
                acc[s, at] = acc[s, at] + got[keep * h + t].astype(jnp.float32)

            base[s] = base[s] + keep * h


def grads_kernel(tiles, x_ref, pre_ref, inv_ref, gain_ref, blocks_ref, where_ref, out_ref,
                 held, dense, scaled, total):
    step = pl.program_id(0)
    pairs = blocks_ref.shape[0]
    width = pairs * LANES

    @pl.when(step == 0)
    def _():
        total[...] = jnp.zeros_like(total)
        held[:, MOSTR] = jnp.zeros((pairs, BLK, LANES), jnp.bfloat16)

    @pl.when(step < tiles)
    def _():
        held[:, :MOSTR] = blocks_ref[...]
        lane = lax.broadcasted_iota(jnp.int32, (BLK, LANES), 1)
        for p in range(pairs):
            row = (step * pairs + p) * 2
            for c in range(KVW // BLK):
                a = held[p, where_ref[row, c]]
                b = held[p, where_ref[row + 1, c]]
                dense[c * BLK:(c + 1) * BLK, p * LANES:(p + 1) * LANES] = jnp.where(
                    lane < BLK, a, b)
        grad = lax.dot_general(
            pre_ref[...], dense[...], (((1,), (0,)), ((), ())),
            preferred_element_type=jnp.float32,
        ) * gain_ref[...]
        scaled[step] = grad
        prod = grad * x_ref[...].astype(jnp.float32)
        part = prod[:, :LANES]
        for j in range(1, width // LANES):
            part = part + prod[:, j * LANES:(j + 1) * LANES]
        total[...] += part

    @pl.when(step == tiles - 1)
    def _():
        inv = inv_ref[:, :1]
        mean = jnp.sum(total[...], axis=1, keepdims=True) / D
        total[...] = jnp.broadcast_to(inv * inv * inv * mean, total.shape)

    @pl.when(step >= tiles)
    def _():
        inv = inv_ref[:, :1]
        back = total[:, :1]
        out_ref[...] = (
            inv * scaled[step - tiles] - back * x_ref[...].astype(jnp.float32)
        ).astype(jnp.bfloat16)


def shards(checkpoint, norm_gain, key_cotangent, positions, kept_cols, kept_count, key_blocks):
    tokens = checkpoint.shape[0]
    dp, seq = lax.axis_size("dp"), lax.axis_size("seq")
    row_blocks, col_blocks = D // BLK, KVW // BLK
    rows_dp = row_blocks // dp
    part = BLK // seq
    half = dp * seq // 2
    slab = rows_dp * part
    gain = norm_gain.reshape(1, D)

    swapped = (
        key_blocks.reshape(rows_dp // 2, 2, MOSTR, BLK, BLK)
        .transpose(0, 2, 4, 1, 3)
        .reshape(rows_dp // 2, MOSTR, BLK, LANES)
    )
    blocks = lax.all_gather(swapped, "dp", axis=0, tiled=True)

    freqs = 10000.0 ** (-2.0 * jnp.arange(HEAD_DIM // 2).astype(jnp.float32) / HEAD_DIM)
    angle = positions.astype(jnp.float32)[:, None] * freqs[None, :]
    cosine, sine = jnp.cos(angle), jnp.sin(angle)
    cosine = jnp.concatenate([cosine, cosine], axis=1)
    sine = jnp.concatenate([sine, -sine], axis=1)

    stages = bits_of(dp) + bits_of(seq)
    vmem = pl.BlockSpec(memory_space=pltpu.VMEM)
    smem = pl.BlockSpec(memory_space=pltpu.SMEM)
    pre, inv, fin = pl.pallas_call(
        functools.partial(sums_kernel, dp, seq),
        out_shape=(
            jax.ShapeDtypeStruct((tokens, KVW), jnp.bfloat16),
            jax.ShapeDtypeStruct((tokens, LANES), jnp.float32),
            jax.ShapeDtypeStruct((STREAMS, slab, LANES), jnp.float32),
        ),
        in_specs=[vmem] * 5 + [smem],
        out_specs=(vmem, vmem, vmem),
        scratch_shapes=[
            pltpu.VMEM((KVW // LANES, rows_dp * BLK, LANES), jnp.float32),
            pltpu.VMEM((STREAMS, half, slab, LANES), jnp.bfloat16),
            pltpu.VMEM((STREAMS, half, slab, LANES), jnp.float32),
            pltpu.VMEM((STREAMS, half, slab, LANES), jnp.bfloat16),
            pltpu.VMEM((STREAMS, half, slab, LANES), jnp.bfloat16),
            pltpu.VMEM((STREAMS, half, slab, LANES), jnp.bfloat16),
            pltpu.SemaphoreType.DMA((STREAMS, stages)),
            pltpu.SemaphoreType.DMA((STREAMS, stages)),
        ],
        compiler_params=pltpu.CompilerParams(
            collective_id=0, has_side_effects=True, vmem_limit_bytes=VMEM),
        cost_estimate=pl.CostEstimate(
            flops=2 * tokens * D * KVW, bytes_accessed=2 * tokens * D, transcendentals=0),
        name="sums",
    )(checkpoint, gain, key_cotangent, cosine, sine, kept_cols)

    live = lax.broadcasted_iota(jnp.int32, (row_blocks, MOSTR), 1) < kept_count[:, None]
    match = (kept_cols[:, :, None] == jnp.arange(col_blocks)[None, None, :]) & live[:, :, None]
    slot = lax.broadcasted_iota(jnp.int32, (row_blocks, MOSTR, col_blocks), 1)
    where = jnp.min(jnp.where(match, slot, MOSTR), axis=1)

    width = 512
    tiles = D // width
    pairs = width // LANES
    grads = pl.pallas_call(
        functools.partial(grads_kernel, tiles),
        grid=(2 * tiles,),
        out_shape=jax.ShapeDtypeStruct((tokens, D), jnp.bfloat16),
        in_specs=[
            pl.BlockSpec((tokens, width), lambda i: (0, i % tiles)),
            pl.BlockSpec((tokens, KVW), lambda i: (0, 0)),
            pl.BlockSpec((tokens, LANES), lambda i: (0, 0)),
            pl.BlockSpec((1, width), lambda i: (0, i % tiles)),
            pl.BlockSpec((pairs, MOSTR, BLK, LANES),
                         lambda i: (jnp.minimum(i, tiles - 1), 0, 0, 0)),
            smem,
        ],
        out_specs=pl.BlockSpec((tokens, width), lambda i: (0, jnp.maximum(i - tiles, 0))),
        scratch_shapes=[
            pltpu.VMEM((pairs, MOSTR + 1, BLK, LANES), jnp.bfloat16),
            pltpu.VMEM((KVW, width), jnp.bfloat16),
            pltpu.VMEM((tiles, tokens, width), jnp.float32),
            pltpu.VMEM((tokens, LANES), jnp.float32),
        ],
        compiler_params=pltpu.CompilerParams(vmem_limit_bytes=VMEM),
        cost_estimate=pl.CostEstimate(
            flops=2 * tokens * D * KVW, bytes_accessed=6 * tokens * D, transcendentals=0),
        name="grads",
    )(checkpoint, pre, inv, gain, blocks, where)

    mine = lax.dynamic_slice_in_dim(live, lax.axis_index("dp") * rows_dp, rows_dp, 0)
    shaped = (
        fin.reshape(STREAMS, rows_dp, part, 2, BLK)
        .transpose(1, 0, 3, 2, 4)
        .reshape(rows_dp, MOSTR, part * BLK)
    )
    divisor = math.sqrt(SEQ_LEN * dp)
    block_grad = jnp.where(mine[:, :, None], shaped / divisor, jnp.float32(0.0))
    return grads, block_grad


def solution(mesh):
    placed = (
        P(("dp", "seq"), None),
        P(),
        P(("dp", "seq"), None),
        P(("dp", "seq")),
        P(),
        P(),
        P("dp", None, None),
    )
    return jax.shard_map(
        shards,
        mesh=mesh,
        in_specs=placed,
        out_specs=(P(("dp", "seq"), None), P("dp", None, "seq")),
        check_vma=False,
    )
```

time: 594 us -> 149 us (0.25)
  waiting for transfers between devices: 281 us -> 0.02 us
  local copies, waits for them, and re-layouts: 209 us -> 6.55 us
  Pallas kernels: 0 us -> 121 us
  matrix products: 52.3 us -> 0 us
  other arithmetic: 24.4 us -> 5.92 us
  starting transfers between devices: 7.2 us -> 0.04 us
    pallas_call x0 -> x2, Pallas kernels: none -> 121 us  [the longest x1 88.4 us: shards(): pl.pallas_call(functools.partial(sums_kernel, dp, seq), out_shape=(jax.Sh...]
    all_to_all x1 -> x0, waiting for transfers between devices: 114 us -> none  [shards(): lax.all_to_all(split_normed, 'seq', split_axis=1, concat_axis=0, tiled=True)]
    reduce_scatter x1 -> x0, waiting for transfers between devices: 102 us -> none  [shards(): lax.psum_scatter(jnp.where(live[:, :, None], picked / divisor, jnp.float3...]
    all_gather x2 -> x1, waiting for transfers between devices: 62.6 us -> 0.01 us  [shards(): blocks = lax.all_gather(swapped, 'dp', axis=0, tiled=True)]
    transpose x3 -> x0, local copies, waits for them, and re-layouts: 60.8 us -> none  [the longest x1 46 us: densify(): placed.reshape(count_rows, col_blocks, rows, BLK).transpose(0, 2, 1, 3)]
    reshape x2 -> x3, local copies, waits for them, and re-layouts: 62.4 us -> 3.47 us  [the longest x2 2.37 us: shards(): key_blocks.reshape(rows_dp // 2, 2, MOSTR, BLK, BLK)]
    dot_general x3 -> x0, matrix products: 52.3 us -> none  [the longest x1 18.8 us: shards(): lax.dot_general(grad_pre, dense, (((1,), (1,)), ((), ())), preferred_elem...]
    dot_general x2 -> x0, local copies, waits for them, and re-layouts: 34.4 us -> none  [the longest x1 22.5 us: densify(): lax.dot_general(onehot, blocks, (((1,), (1,)), ((0,), (0,))), preferred_e...]
  transfers between devices with their start and end apart: 4 -> 1, of which waited for: 3 -> 0; matrix products, arithmetic and copies ran while one was open for 5% -> 6% of each run, Pallas kernels for 0% -> 60%
where the time goes in v1:
time: 149 us; the launch traced here: 148 us
  Pallas kernels  121 us (81%)
  between operations  14.1 us (9%)
  local copies, waits for them, and re-layouts  6.55 us (4%)
  other arithmetic  5.92 us (4%)
    pallas_call x1, Pallas kernels, shards(): pl.pallas_call(functools.partial(sums_kernel, dp, seq), out_shape=(jax.Sh...  88.4 us
    pallas_call x1, Pallas kernels, shards(): pl.pallas_call(functools.partial(grads_kernel, tiles), grid=(2 * tiles,),...  32.7 us
  transfers between devices with their start and end apart: 1, of which 0 were waited for; matrix products, arithmetic and copies ran while one was open for 6% of the time, Pallas kernels for 60%

profile of v1, /device:TPU:0, one launch (start us, length us, event | category | flops | bytes accessed | tf_op | source)
XLA Modules:
  0.0 147.7 jit_solution(14521033776241615005)
XLA Ops:
  7.2 0.0 all-gather.2.cloned.1.call-start
  7.2 1.8 %reshape.48 = bf16[4,2,6,64,64]{4,3,1,0,2:T(8,128)(2,1)S(1)} reshape(bf16[8,6,4096]{2,0,1:T(8,128)(2,1)} %param.13) | data formatting | bytes 786432 | tf_op jit(solution)/shard_map/reshape | solution.py:249
  9.0 0.6 copy.20
  9.6 1.1 reshape.49
  10.7 0.0 all-gather.2.cloned.1.call-update
  10.7 0.7 convert_element_type.10
  11.4 1.4 copy.19.cols_ref
  12.8 0.7 iota_compare_fusion.1
  13.5 0.7 select_reduce_fusion
  14.2 0.7 copy.21.where_ref
  14.9 1.0 multiply_sine_fusion
  15.9 1.0 pad_maximum_fusion
  16.9 88.4 %sums.1 = (bf16[512,1024]{1,0:T(8,128)(2,1)}, f32[512,128]{1,0:T(8,128)}, f32[3,256,128]{2,1,0:T(8,128)}) custom-call(bf16[512,8192]{1,0:T(8,128)(2,1)} %x_ref.3, f32[1,8192]{1,0:T(1,128)} %bitcast.11, bf16[512,1024]{1,0:T(8,128)(2,1)} %cot_ref.1, f32[512,128]{1,0:T(8,128)} %get-tuple-element.11.cos_ref, f32[512,128]{1,0:T(8,128)} %get-tuple-element.12.sin_ref, ...), custom_call_target="tpu_custom_call" | custom-call | flops 8589934592 | bytes 8388608 | tf_op jit(solution)/shard_map/sums/pallas_call | solution.py:264
  105.3 1.0 broadcast_multiply_fusion
  106.4 0.5 div.22
  106.8 0.1 copy.22
  106.9 0.3 div.24
  107.2 0.1 constant_dynamic-slice_fusion
  107.3 0.8 broadcast_select_fusion
  108.2 0.0 all-gather.2.cloned.1.call-done.blocks_ref
  108.2 32.7 %grads.1 = bf16[512,8192]{1,0:T(8,128)(2,1)} custom-call(bf16[512,8192]{1,0:T(8,128)(2,1)} %x_ref.3, bf16[512,1024]{1,0:T(8,128)(2,1)} %get-tuple-element.5.pre_ref, f32[512,128]{1,0:T(8,128)} %get-tuple-element.6.inv_ref, f32[1,8192]{1,0:T(1,128)} %bitcast.12, bf16[64,6,64,128]{3,2,1,0:T(8,128)(2,1)} %all-gather.2.cloned.1.call-done.blocks_ref, ...), custom_call_target="tpu_custom_call" | custom-call | flops 8589934592 | bytes 25165824 | tf_op jit(solution)/shard_map/grads/pallas_call | solution.py:298
  (1 shorter events, 0.0 us)
Async XLA Ops:
  7.2 101.0 %all-gather.2.cloned.1.call-start = ((), (), s32[]{:S(2)}) async-start(), calls=%async_computation | async-start | bytes 6684672 | tf_op jit(solution)/shard_map/all_gather | solution.py:253
Sparse Core Ops, SparseCore 0:
  10.9 85.9 all-gather.1

commit v2 on v1

--- a/solution.py
+++ b/solution.py
@@ -45,9 +45,18 @@
     return place
 
 
-def sums_kernel(dp, seq, x_ref, gain_ref, cot_ref, cos_ref, sin_ref, cols_ref,
-                pre_ref, inv_ref, fin_ref,
-                sums, first, acc, later, recv_first, recv_later, send_sem, recv_sem):
+def gather_plan(dp, seq):
+    steps = [("dp", b) for b in reversed(range(bits_of(dp)))]
+    if seq == 2:
+        swap = steps[:-1] + [("seq", 0)] + steps[-1:]
+        return [steps, swap, swap]
+    return [steps] * STREAMS
+
+
+def sums_kernel(dp, seq, x_ref, gain_ref, cot_ref, cos_ref, sin_ref, cols_ref, own_ref,
+                pre_ref, inv_ref, fin_ref, all_ref,
+                sums, first, acc, later, recv_first, recv_later, send_sem, recv_sem,
+                gather_send, gather_recv, local_sem):
     tokens = x_ref.shape[0]
     rows_dp = (D // BLK) // dp
     part = BLK // seq
@@ -70,6 +79,42 @@
         pl.semaphore_signal(barrier, inc=1, device_id=partner(axis, b),
                             device_id_type=pl.DeviceIdType.MESH)
     pl.semaphore_wait(barrier, stages)
+
+    steps = gather_plan(dp, seq)
+
+    def slots(s, i):
+        split = ("seq", 0) in steps[s]
+        if not split or i > steps[s].index(("seq", 0)):
+            return pl.ds(2 * s, 2)
+        return pl.ds(2 * s + me_seq, 1)
+
+    def gather(s, i):
+        axis, b = steps[s][i]
+        n = 1 << sum(1 for a, _ in steps[s][:i] if a == "dp")
+        src = own_ref if i == 0 else all_ref.at[pl.ds(0, n)]
+        dst = all_ref.at[pl.ds(n, n) if axis == "dp" else pl.ds(0, n)]
+        return pltpu.make_async_remote_copy(
+            src_ref=src.at[:, slots(s, i)], dst_ref=dst.at[:, slots(s, i)],
+            send_sem=gather_send.at[s, i], recv_sem=gather_recv.at[s, i],
+            device_id=partner(axis, b), device_id_type=pl.DeviceIdType.MESH,
+        )
+
+    def keep_own(s):
+        return pltpu.make_async_copy(
+            own_ref.at[:, slots(s, 0)], all_ref.at[pl.ds(0, 1), slots(s, 0)], local_sem.at[s])
+
+    def advance(s, i):
+        if i >= len(steps[s]):
+            return
+        if i == 0:
+            keep_own(s).wait()
+        gather(s, i).wait()
+        if i + 1 < len(steps[s]):
+            gather(s, i + 1).start()
+
+    for s in (1, 2, 0):
+        gather(s, 0).start()
+        keep_own(s).start()
 
     tt = 64
 
@@ -89,6 +134,9 @@
             pre_ref[rows, h * HEAD_DIM:(h + 1) * HEAD_DIM] = (
                 v * cosine + pltpu.roll(v, HEAD_DIM // 2, 1) * sine
             ).astype(jnp.bfloat16)
+
+    advance(1, 0)
+    advance(2, 0)
 
     lane = lax.broadcasted_iota(jnp.int32, (BLK, LANES), 1)
 
@@ -143,6 +191,21 @@
 
         one_owner(2 * o + 1 - mine, store)
 
+        @pl.when(o == (dp // 2) // 8)
+        def _():
+            advance(0, 0)
+            advance(1, 1)
+            advance(2, 1)
+
+        @pl.when(o == 4 * (dp // 2) // 8)
+        def _():
+            advance(0, 1)
+            advance(1, 2)
+
+        @pl.when(o == 6 * (dp // 2) // 8)
+        def _():
+            advance(2, 2)
+
     copies = {}
     for s in range(STREAMS):
         copies[s, 0] = exchange(s, 0, half)
@@ -155,6 +218,16 @@
 
         one_owner(2 * o + mine, store)
 
+        @pl.when(o == 3 * (dp // 2) // 8)
+        def _():
+            advance(0, 2)
+            advance(1, 3)
+
+        @pl.when(o == 7 * (dp // 2) // 8)
+        def _():
+            advance(2, 3)
+
+    done = [3, 4, 4]
     base = [0] * STREAMS
     for i in range(stages):
         size = half >> i
@@ -185,28 +258,32 @@
                 acc[s, at] = acc[s, at] + got[keep * h + t].astype(jnp.float32)
 
             base[s] = base[s] + keep * h
-
-
-def grads_kernel(tiles, x_ref, pre_ref, inv_ref, gain_ref, blocks_ref, where_ref, out_ref,
-                 held, dense, scaled, total):
+        for s in range(STREAMS):
+            if i == stages - 2:
+                for k in range(done[s], len(steps[s])):
+                    advance(s, k)
+
+
+def grads_kernel(tiles, place_ref, x_ref, pre_ref, inv_ref, gain_ref, blocks_ref, where_ref,
+                 out_ref, held, dense, scaled, total):
     step = pl.program_id(0)
-    pairs = blocks_ref.shape[0]
+    pairs = blocks_ref.shape[2] // BLK
     width = pairs * LANES
 
     @pl.when(step == 0)
     def _():
         total[...] = jnp.zeros_like(total)
-        held[:, MOSTR] = jnp.zeros((pairs, BLK, LANES), jnp.bfloat16)
+        held[MOSTR] = jnp.zeros((pairs * BLK, LANES), jnp.bfloat16)
 
     @pl.when(step < tiles)
     def _():
-        held[:, :MOSTR] = blocks_ref[...]
+        held[:MOSTR] = blocks_ref[0]
         lane = lax.broadcasted_iota(jnp.int32, (BLK, LANES), 1)
         for p in range(pairs):
             row = (step * pairs + p) * 2
             for c in range(KVW // BLK):
-                a = held[p, where_ref[row, c]]
-                b = held[p, where_ref[row + 1, c]]
+                a = held[where_ref[row, c], p * BLK:(p + 1) * BLK]
+                b = held[where_ref[row + 1, c], p * BLK:(p + 1) * BLK]
                 dense[c * BLK:(c + 1) * BLK, p * LANES:(p + 1) * LANES] = jnp.where(
                     lane < BLK, a, b)
         grad = lax.dot_general(
@@ -247,10 +324,9 @@
 
     swapped = (
         key_blocks.reshape(rows_dp // 2, 2, MOSTR, BLK, BLK)
-        .transpose(0, 2, 4, 1, 3)
-        .reshape(rows_dp // 2, MOSTR, BLK, LANES)
+        .transpose(2, 0, 4, 1, 3)
+        .reshape(1, MOSTR, rows_dp // 2 * BLK, LANES)
     )
-    blocks = lax.all_gather(swapped, "dp", axis=0, tiled=True)
 
     freqs = 10000.0 ** (-2.0 * jnp.arange(HEAD_DIM // 2).astype(jnp.float32) / HEAD_DIM)
     angle = positions.astype(jnp.float32)[:, None] * freqs[None, :]
@@ -261,15 +337,17 @@
     stages = bits_of(dp) + bits_of(seq)
     vmem = pl.BlockSpec(memory_space=pltpu.VMEM)
     smem = pl.BlockSpec(memory_space=pltpu.SMEM)
-    pre, inv, fin = pl.pallas_call(
+    anywhere = pl.BlockSpec(memory_space=pl.ANY)
+    pre, inv, fin, blocks = pl.pallas_call(
         functools.partial(sums_kernel, dp, seq),
         out_shape=(
             jax.ShapeDtypeStruct((tokens, KVW), jnp.bfloat16),
             jax.ShapeDtypeStruct((tokens, LANES), jnp.float32),
             jax.ShapeDtypeStruct((STREAMS, slab, LANES), jnp.float32),
+            jax.ShapeDtypeStruct((dp,) + swapped.shape[1:], jnp.bfloat16),
         ),
-        in_specs=[vmem] * 5 + [smem],
-        out_specs=(vmem, vmem, vmem),
+        in_specs=[vmem] * 5 + [smem, anywhere],
+        out_specs=(vmem, vmem, vmem, anywhere),
         scratch_shapes=[
             pltpu.VMEM((KVW // LANES, rows_dp * BLK, LANES), jnp.float32),
             pltpu.VMEM((STREAMS, half, slab, LANES), jnp.bfloat16),
@@ -279,47 +357,59 @@
             pltpu.VMEM((STREAMS, half, slab, LANES), jnp.bfloat16),
             pltpu.SemaphoreType.DMA((STREAMS, stages)),
             pltpu.SemaphoreType.DMA((STREAMS, stages)),
+            pltpu.SemaphoreType.DMA((STREAMS, stages)),
+            pltpu.SemaphoreType.DMA((STREAMS, stages)),
+            pltpu.SemaphoreType.DMA((STREAMS,)),
         ],
         compiler_params=pltpu.CompilerParams(
             collective_id=0, has_side_effects=True, vmem_limit_bytes=VMEM),
         cost_estimate=pl.CostEstimate(
             flops=2 * tokens * D * KVW, bytes_accessed=2 * tokens * D, transcendentals=0),
         name="sums",
-    )(checkpoint, gain, key_cotangent, cosine, sine, kept_cols)
+    )(checkpoint, gain, key_cotangent, cosine, sine, kept_cols, swapped)
 
     live = lax.broadcasted_iota(jnp.int32, (row_blocks, MOSTR), 1) < kept_count[:, None]
     match = (kept_cols[:, :, None] == jnp.arange(col_blocks)[None, None, :]) & live[:, :, None]
     slot = lax.broadcasted_iota(jnp.int32, (row_blocks, MOSTR, col_blocks), 1)
     where = jnp.min(jnp.where(match, slot, MOSTR), axis=1)
 
-    width = 512
-    tiles = D // width
+    differs = jnp.bitwise_xor(jnp.arange(dp, dtype=jnp.int32), lax.axis_index("dp"))
+    place = jnp.zeros((dp,), jnp.int32)
+    for b in range(bits_of(dp)):
+        place = place * 2 + bit(differs, b)
+
+    width = rows_dp * BLK
+    tiles = dp
     pairs = width // LANES
     grads = pl.pallas_call(
         functools.partial(grads_kernel, tiles),
-        grid=(2 * tiles,),
+        grid_spec=pltpu.PrefetchScalarGridSpec(
+            num_scalar_prefetch=1,
+            grid=(2 * tiles,),
+            in_specs=[
+                pl.BlockSpec((tokens, width), lambda i, place: (0, i % tiles)),
+                pl.BlockSpec((tokens, KVW), lambda i, place: (0, 0)),
+                pl.BlockSpec((tokens, LANES), lambda i, place: (0, 0)),
+                pl.BlockSpec((1, width), lambda i, place: (0, i % tiles)),
+                pl.BlockSpec((1, MOSTR, pairs * BLK, LANES),
+                             lambda i, place: (place[jnp.minimum(i, tiles - 1)], 0, 0, 0)),
+                smem,
+            ],
+            out_specs=pl.BlockSpec(
+                (tokens, width), lambda i, place: (0, jnp.maximum(i - tiles, 0))),
+            scratch_shapes=[
+                pltpu.VMEM((MOSTR + 1, pairs * BLK, LANES), jnp.bfloat16),
+                pltpu.VMEM((KVW, width), jnp.bfloat16),
+                pltpu.VMEM((tiles, tokens, width), jnp.float32),
+                pltpu.VMEM((tokens, LANES), jnp.float32),
+            ],
+        ),
         out_shape=jax.ShapeDtypeStruct((tokens, D), jnp.bfloat16),
-        in_specs=[
-            pl.BlockSpec((tokens, width), lambda i: (0, i % tiles)),
-            pl.BlockSpec((tokens, KVW), lambda i: (0, 0)),
-            pl.BlockSpec((tokens, LANES), lambda i: (0, 0)),
-            pl.BlockSpec((1, width), lambda i: (0, i % tiles)),
-            pl.BlockSpec((pairs, MOSTR, BLK, LANES),
-                         lambda i: (jnp.minimum(i, tiles - 1), 0, 0, 0)),
-            smem,
-        ],
-        out_specs=pl.BlockSpec((tokens, width), lambda i: (0, jnp.maximum(i - tiles, 0))),
-        scratch_shapes=[
-            pltpu.VMEM((pairs, MOSTR + 1, BLK, LANES), jnp.bfloat16),
-            pltpu.VMEM((KVW, width), jnp.bfloat16),
-            pltpu.VMEM((tiles, tokens, width), jnp.float32),
-            pltpu.VMEM((tokens, LANES), jnp.float32),
-        ],
         compiler_params=pltpu.CompilerParams(vmem_limit_bytes=VMEM),
         cost_estimate=pl.CostEstimate(
             flops=2 * tokens * D * KVW, bytes_accessed=6 * tokens * D, transcendentals=0),
         name="grads",
-    )(checkpoint, pre, inv, gain, blocks, where)
+    )(place, checkpoint, pre, inv, gain, blocks, where)
 
     mine = lax.dynamic_slice_in_dim(live, lax.axis_index("dp") * rows_dp, rows_dp, 0)
     shaped = (

time: 149 us -> 141 us (0.946)
  between operations: 14.1 us -> 0.69 us
  Pallas kernels: 121 us -> 126 us
    pallas_call x1, Pallas kernels: 88.4 us -> 92.7 us  [shards(): pl.pallas_call(functools.partial(sums_kernel, dp, seq), out_shape=(jax.Sh...]
  transfers between devices with their start and end apart: 1 -> 0, of which waited for: 0 -> 0; matrix products, arithmetic and copies ran while one was open for 6% -> 0% of each run, Pallas kernels for 60% -> 0%
where the time goes in v2:
time: 141 us; the launch traced here: 140 us
  Pallas kernels  126 us (89%)
  local copies, waits for them, and re-layouts  6.56 us (5%)
  other arithmetic  6.45 us (5%)
    pallas_call x1, Pallas kernels, shards(): pl.pallas_call(functools.partial(sums_kernel, dp, seq), out_shape=(jax.Sh...  92.7 us
    pallas_call x1, Pallas kernels, shards(): pl.pallas_call(functools.partial(grads_kernel, tiles), grid_spec=pltpu.Pr...  33.4 us

profile of v2, /device:TPU:0, one launch (start us, length us, event | category | flops | bytes accessed | tf_op | source)
XLA Modules:
  0.0 139.8 jit_solution(3954332091776986738)
XLA Ops:
  0.6 0.5 fusion.4.place_ref
  1.2 0.7 iota_compare_fusion.1
  1.9 0.1 constant_dynamic-slice_fusion
  1.9 0.7 convert_element_type.10
  2.6 0.7 select_reduce_fusion
  3.3 0.8 copy.16.where_ref
  4.1 1.4 %copy.15.cols_ref = s32[128,6]{1,0:T(8,128)} copy(s32[128,6]{0,1:T(8,128)} %param.11) | data formatting | bytes 6144 | tf_op args[4]
  5.5 1.0 multiply_sine_fusion
  6.5 1.0 pad_maximum_fusion
  7.5 1.8 %reshape.48 = bf16[4,2,6,64,64]{4,3,1,0,2:T(8,128)(2,1)S(1)} reshape(bf16[8,6,4096]{2,0,1:T(8,128)(2,1)} %param.13) | data formatting | bytes 786432 | tf_op jit(solution)/shard_map/reshape | solution.py:326
  9.2 0.6 copy.14
  9.9 1.1 reshape.49.own_ref
  11.0 92.7 %sums.1 = (bf16[512,1024]{1,0:T(8,128)(2,1)}, f32[512,128]{1,0:T(8,128)}, f32[3,256,128]{2,1,0:T(8,128)}, bf16[16,6,256,128]{3,2,1,0:T(8,128)(2,1)}) custom-call(bf16[512,8192]{1,0:T(8,128)(2,1)} %x_ref.3, f32[1,8192]{1,0:T(1,128)} %bitcast.11, bf16[512,1024]{1,0:T(8,128)(2,1)} %cot_ref.1, f32[512,128]{1,0:T(8,128)} %get-tuple-element.13.cos_ref, ...), custom_call_target="tpu_custom_call" | custom-call | flops 8589934592 | bytes 8388608 | tf_op jit(solution)/shard_map/sums/pallas_call | solution.py:341
  103.7 1.0 broadcast_multiply_fusion
  104.7 0.5 div.59
  105.2 0.1 copy.17
  105.3 0.3 div.61
  105.6 0.8 broadcast_select_fusion
  106.4 33.4 %grads.1 = bf16[512,8192]{1,0:T(8,128)(2,1)} custom-call(s32[16]{0:T(128)} %fusion.4.place_ref, bf16[512,8192]{1,0:T(8,128)(2,1)} %x_ref.3, bf16[512,1024]{1,0:T(8,128)(2,1)} %get-tuple-element.6.pre_ref, f32[512,128]{1,0:T(8,128)} %get-tuple-element.7.inv_ref, f32[1,8192]{1,0:T(1,128)} %bitcast.12, bf16[16,6,256,128]{3,2,1,0:T(8,128)(2,1)} %get-tuple-element.8.blocks_ref, ...), custom_call_target="tpu_custom_call" | custom-call | flops 8589934592 | bytes 25165824 | tf_op jit(solution)/shard_map/grads/pallas_call | solution.py:384
  (1 shorter events, 0.0 us)
